TPU v7x, 32 devices: a whole 2x2x4 slice. The times are simulated.
32 devices in a mesh: pair: 2 (over x), vblk: 16 (over z, y, core).
Axes of the slice: x: 2, y: 2, z: 4, core: 2. Of those that a mesh axis runs over, the one named last changes fastest.
Arguments:
- factors: bfloat16 [1536, 80, 512], P('pair', 'vblk'), may hold values from -2.5 to 2.5
- amplitudes: bfloat16 [8, 512, 512], P(None, ('pair', 'vblk')), may hold values from -0.01171875 to 0.01171875
Outputs:
- ladder: float32 [8, 80, 2, 5], P('pair', 'vblk')
All inputs are finite; a program needn't handle non-finite values.
Results may differ from a plain program's by a relative error of at most 0.0003.
Values may be sent and summed in bfloat16 or wider, within the bound.
A program may use at most 64 MiB of HBM per device.

v0:
```python
import math

import jax
import jax.numpy as jnp
from jax import lax
from jax.sharding import PartitionSpec as P

STEPS = 2


def shifted(value, axis, steps):
    count = lax.axis_size(axis)
    pairs = [(source, (source + steps) % count) for source in range(count)]
    return lax.ppermute(value, axis, pairs)


def body(factors, amplitudes):
    aux_rows = factors.shape[0]
    block_rows = factors.shape[1]
    pair_count = amplitudes.shape[0]
    virtuals = amplitudes.shape[2]
    collected = [factors]
    current = factors
    current = shifted(current, "vblk", 1)
    collected.append(current)
    partner = jnp.concatenate(collected, axis=1)
    initial = jnp.zeros((pair_count, block_rows, STEPS * block_rows), jnp.float32)
    running = initial
    amp_piece = lax.all_gather(amplitudes, ("pair", "vblk"), axis=1, tiled=True)
    row_count = amp_piece.shape[1]
    group_size = math.gcd(row_count, 64)
    block_count = row_count // group_size
    piece_blocks = amp_piece.reshape(pair_count, block_count, group_size, virtuals).transpose(
        1, 0, 2, 3
    )
    own_parts = factors.reshape(aux_rows, block_rows, block_count, group_size).transpose(2, 0, 1, 3)

    def one_block(carried, pieces):
        piece_part, own_part = pieces
        integrals = jnp.einsum(
            "qac,qbd->acbd", own_part, partner, preferred_element_type=jnp.float32
        )
        update = jnp.einsum(
            "pcd,acbd->pab",
            piece_part.astype(jnp.float32),
            integrals,
            precision=lax.Precision.HIGHEST,
        )
        return (carried + update, None)

    running, unused = lax.scan(one_block, running, (piece_blocks, own_parts))
    partial_ladder = running
    partial_ladder = partial_ladder.reshape(pair_count, block_rows, STEPS, block_rows)
    return lax.psum_scatter(partial_ladder, "pair", scatter_dimension=0, tiled=True)


def solution(mesh):
    placed = (P("pair", "vblk", None), P(None, ("pair", "vblk"), None))
    return jax.shard_map(
        body, mesh=mesh, in_specs=placed, out_specs=P("pair", "vblk", None, None), check_vma=False
    )
```

profile of v0, /device:TPU:15, one launch (start us, length us, event | category | flops | bytes accessed | tf_op | source)
XLA Modules:
  0.0 344.6 jit_solution(10008234704764163319)
XLA Ops:
  6.5 0.0 copy-start
  6.5 0.0 all-gather.2.cloned.1.call-start
  6.5 0.7 all-gather.2.cloned.1.call-update
  7.3 1.9 collective-permute-start
  9.1 6.3 %copy.15 = bf16[768,5,512]{0,2,1:T(8,128)(2,1)} copy(bf16[768,5,512]{2,0,1:T(8,128)(2,1)} %param.4) | data formatting | bytes 7864320 | tf_op args[0]
  15.4 0.0 copy-done
  15.4 0.7 dynamic-slice
  16.8 37.9 %collective-permute-done = bf16[768,5,512]{2,0,1:T(8,128)(2,1)} collective-permute-done((bf16[768,5,512]{2,0,1:T(8,128)(2,1)}, bf16[768,5,512]{2,0,1:T(8,128)(2,1)}, u32[]{:S(2)}, u32[]{:S(2)}) %collective-permute-start) | collective-permute-done | bytes 3932192 | tf_op jit(solution)/shard_map/ppermute | solution.py:14
  54.7 7.1 %pad_maximum_fusion = bf16[768,10,512]{2,0,1:T(8,128)(2,1)} fusion(bf16[768,5,512]{2,0,1:T(8,128)(2,1)} %collective-permute-done, bf16[768,5,512]{2,0,1:T(8,128)(2,1)} %param.4), kind=kLoop, calls=%fused_computation.12 | loop fusion | flops 3932160 | bytes 15728640 | tf_op jit(solution)/shard_map/concatenate | solution.py:26
  61.8 35.5 %all-gather.2.cloned.1.call-done = bf16[8,512,512]{2,1,0:T(8,128)(2,1)} async-done(((bf16[8,16,512]{2,1,0:T(8,128)(2,1)}), bf16[8,512,512]{2,1,0:T(8,128)(2,1)}) %all-gather.2.cloned.1.call-update) | async-done | bytes 4194320 | tf_op jit(solution)/shard_map/all_gather | solution.py:29
  97.2 6.5 %copy.14 = bf16[8,512,512]{2,0,1:T(8,128)(2,1)} copy(bf16[8,512,512]{2,1,0:T(8,128)(2,1)} %all-gather.2.cloned.1.call-done) | data formatting | bytes 8388608 | tf_op jit(solution)/shard_map/all_gather | solution.py:29
  103.7 226.8 %while.11 = (s32[]{:T(128)}, f32[8,5,10]{2,0,1:T(8,128)S(1)}, bf16[8,8,64,512]{3,1,2,0:T(8,128)(2,1)}, bf16[8,768,5,64]{1,3,0,2:T(8,128)(2,1)}, bf16[768,10,512]{2,0,1:T(8,128)(2,1)}, /*index=5*/s32[]{:T(128)}, s32[]{:T(128)}) while((s32[]{:T(128)}, f32[8,5,10]{2,0,1:T(8,128)S(1)}, bf16[8,8,64,512]{3,1,2,0:T(8,128)(2,1)}, ...), condition=%wide.region_1.2_spmd.clone, body=%wide.region_0.1_spmd.clone.sunk | while | flops 2673869568 | bytes 21991640 | solution.py:51
  103.7 8.9 %fusion.26 = f32[5,64,10,512]{3,1,2,0:T(8,128)} fusion(bf16[768,10,512]{2,0,1:T(8,128)(2,1)} %get-tuple-element.120, bf16[8,768,5,64]{1,3,0,2:T(8,128)(2,1)} %get-tuple-element.119, s32[]{:T(128)} %get-tuple-element.109), kind=kOutput, calls=%fused_computation.2.clone.1 | convolution fusion | flops 2516582400 | bytes 14909952 | tf_op jit(solution)/shard_map/while/body/eval_jaxpr/qac,qbd->acbd/dot_general | solution.py:40
  112.7 19.4 %fusion.27 = f32[8,5,10]{2,0,1:T(8,128)S(1)} fusion(f32[5,64,10,512]{3,1,2,0:T(8,128)} %fusion.26, bf16[8,8,64,512]{3,1,2,0:T(8,128)(2,1)} %get-tuple-element.118, s32[]{:T(128)} %get-tuple-element.109, f32[8,5,10]{2,0,1:T(8,128)S(1)} %get-tuple-element.110, pred[]{:T(512)S(6)} %compare.3), kind=kOutput, calls=%fused_computation.5.clone.1 | convolution fusion | flops 157287200 | bytes 7081601 | tf_op jit(solution)/shard_map/while/body/eval_jaxpr/pcd,acbd->pab/dot_general | solution.py:43
  132.1 8.9 %fusion.26 = f32[5,64,10,512]{3,1,2,0:T(8,128)} fusion(bf16[768,10,512]{2,0,1:T(8,128)(2,1)} %get-tuple-element.120, bf16[8,768,5,64]{1,3,0,2:T(8,128)(2,1)} %get-tuple-element.119, s32[]{:T(128)} %get-tuple-element.109), kind=kOutput, calls=%fused_computation.2.clone.1 | convolution fusion | flops 2516582400 | bytes 14909952 | tf_op jit(solution)/shard_map/while/body/eval_jaxpr/qac,qbd->acbd/dot_general | solution.py:40
  141.0 19.4 %fusion.27 = f32[8,5,10]{2,0,1:T(8,128)S(1)} fusion(f32[5,64,10,512]{3,1,2,0:T(8,128)} %fusion.26, bf16[8,8,64,512]{3,1,2,0:T(8,128)(2,1)} %get-tuple-element.118, s32[]{:T(128)} %get-tuple-element.109, f32[8,5,10]{2,0,1:T(8,128)S(1)} %get-tuple-element.110, pred[]{:T(512)S(6)} %compare.3), kind=kOutput, calls=%fused_computation.5.clone.1 | convolution fusion | flops 157287200 | bytes 7081601 | tf_op jit(solution)/shard_map/while/body/eval_jaxpr/pcd,acbd->pab/dot_general | solution.py:43
  160.4 8.9 %fusion.26 = f32[5,64,10,512]{3,1,2,0:T(8,128)} fusion(bf16[768,10,512]{2,0,1:T(8,128)(2,1)} %get-tuple-element.120, bf16[8,768,5,64]{1,3,0,2:T(8,128)(2,1)} %get-tuple-element.119, s32[]{:T(128)} %get-tuple-element.109), kind=kOutput, calls=%fused_computation.2.clone.1 | convolution fusion | flops 2516582400 | bytes 14909952 | tf_op jit(solution)/shard_map/while/body/eval_jaxpr/qac,qbd->acbd/dot_general | solution.py:40
  169.4 19.4 %fusion.27 = f32[8,5,10]{2,0,1:T(8,128)S(1)} fusion(f32[5,64,10,512]{3,1,2,0:T(8,128)} %fusion.26, bf16[8,8,64,512]{3,1,2,0:T(8,128)(2,1)} %get-tuple-element.118, s32[]{:T(128)} %get-tuple-element.109, f32[8,5,10]{2,0,1:T(8,128)S(1)} %get-tuple-element.110, pred[]{:T(512)S(6)} %compare.3), kind=kOutput, calls=%fused_computation.5.clone.1 | convolution fusion | flops 157287200 | bytes 7081601 | tf_op jit(solution)/shard_map/while/body/eval_jaxpr/pcd,acbd->pab/dot_general | solution.py:43
  188.8 8.9 %fusion.26 = f32[5,64,10,512]{3,1,2,0:T(8,128)} fusion(bf16[768,10,512]{2,0,1:T(8,128)(2,1)} %get-tuple-element.120, bf16[8,768,5,64]{1,3,0,2:T(8,128)(2,1)} %get-tuple-element.119, s32[]{:T(128)} %get-tuple-element.109), kind=kOutput, calls=%fused_computation.2.clone.1 | convolution fusion | flops 2516582400 | bytes 14909952 | tf_op jit(solution)/shard_map/while/body/eval_jaxpr/qac,qbd->acbd/dot_general | solution.py:40
  197.7 19.4 %fusion.27 = f32[8,5,10]{2,0,1:T(8,128)S(1)} fusion(f32[5,64,10,512]{3,1,2,0:T(8,128)} %fusion.26, bf16[8,8,64,512]{3,1,2,0:T(8,128)(2,1)} %get-tuple-element.118, s32[]{:T(128)} %get-tuple-element.109, f32[8,5,10]{2,0,1:T(8,128)S(1)} %get-tuple-element.110, pred[]{:T(512)S(6)} %compare.3), kind=kOutput, calls=%fused_computation.5.clone.1 | convolution fusion | flops 157287200 | bytes 7081601 | tf_op jit(solution)/shard_map/while/body/eval_jaxpr/pcd,acbd->pab/dot_general | solution.py:43
  217.1 8.9 %fusion.26 = f32[5,64,10,512]{3,1,2,0:T(8,128)} fusion(bf16[768,10,512]{2,0,1:T(8,128)(2,1)} %get-tuple-element.120, bf16[8,768,5,64]{1,3,0,2:T(8,128)(2,1)} %get-tuple-element.119, s32[]{:T(128)} %get-tuple-element.109), kind=kOutput, calls=%fused_computation.2.clone.1 | convolution fusion | flops 2516582400 | bytes 14909952 | tf_op jit(solution)/shard_map/while/body/eval_jaxpr/qac,qbd->acbd/dot_general | solution.py:40
  226.1 19.4 %fusion.27 = f32[8,5,10]{2,0,1:T(8,128)S(1)} fusion(f32[5,64,10,512]{3,1,2,0:T(8,128)} %fusion.26, bf16[8,8,64,512]{3,1,2,0:T(8,128)(2,1)} %get-tuple-element.118, s32[]{:T(128)} %get-tuple-element.109, f32[8,5,10]{2,0,1:T(8,128)S(1)} %get-tuple-element.110, pred[]{:T(512)S(6)} %compare.3), kind=kOutput, calls=%fused_computation.5.clone.1 | convolution fusion | flops 157287200 | bytes 7081601 | tf_op jit(solution)/shard_map/while/body/eval_jaxpr/pcd,acbd->pab/dot_general | solution.py:43
  245.5 8.9 %fusion.26 = f32[5,64,10,512]{3,1,2,0:T(8,128)} fusion(bf16[768,10,512]{2,0,1:T(8,128)(2,1)} %get-tuple-element.120, bf16[8,768,5,64]{1,3,0,2:T(8,128)(2,1)} %get-tuple-element.119, s32[]{:T(128)} %get-tuple-element.109), kind=kOutput, calls=%fused_computation.2.clone.1 | convolution fusion | flops 2516582400 | bytes 14909952 | tf_op jit(solution)/shard_map/while/body/eval_jaxpr/qac,qbd->acbd/dot_general | solution.py:40
  254.4 19.4 %fusion.27 = f32[8,5,10]{2,0,1:T(8,128)S(1)} fusion(f32[5,64,10,512]{3,1,2,0:T(8,128)} %fusion.26, bf16[8,8,64,512]{3,1,2,0:T(8,128)(2,1)} %get-tuple-element.118, s32[]{:T(128)} %get-tuple-element.109, f32[8,5,10]{2,0,1:T(8,128)S(1)} %get-tuple-element.110, pred[]{:T(512)S(6)} %compare.3), kind=kOutput, calls=%fused_computation.5.clone.1 | convolution fusion | flops 157287200 | bytes 7081601 | tf_op jit(solution)/shard_map/while/body/eval_jaxpr/pcd,acbd->pab/dot_general | solution.py:43
  273.8 8.9 %fusion.26 = f32[5,64,10,512]{3,1,2,0:T(8,128)} fusion(bf16[768,10,512]{2,0,1:T(8,128)(2,1)} %get-tuple-element.120, bf16[8,768,5,64]{1,3,0,2:T(8,128)(2,1)} %get-tuple-element.119, s32[]{:T(128)} %get-tuple-element.109), kind=kOutput, calls=%fused_computation.2.clone.1 | convolution fusion | flops 2516582400 | bytes 14909952 | tf_op jit(solution)/shard_map/while/body/eval_jaxpr/qac,qbd->acbd/dot_general | solution.py:40
  282.8 19.4 %fusion.27 = f32[8,5,10]{2,0,1:T(8,128)S(1)} fusion(f32[5,64,10,512]{3,1,2,0:T(8,128)} %fusion.26, bf16[8,8,64,512]{3,1,2,0:T(8,128)(2,1)} %get-tuple-element.118, s32[]{:T(128)} %get-tuple-element.109, f32[8,5,10]{2,0,1:T(8,128)S(1)} %get-tuple-element.110, pred[]{:T(512)S(6)} %compare.3), kind=kOutput, calls=%fused_computation.5.clone.1 | convolution fusion | flops 157287200 | bytes 7081601 | tf_op jit(solution)/shard_map/while/body/eval_jaxpr/pcd,acbd->pab/dot_general | solution.py:43
  302.2 8.9 %fusion.26 = f32[5,64,10,512]{3,1,2,0:T(8,128)} fusion(bf16[768,10,512]{2,0,1:T(8,128)(2,1)} %get-tuple-element.120, bf16[8,768,5,64]{1,3,0,2:T(8,128)(2,1)} %get-tuple-element.119, s32[]{:T(128)} %get-tuple-element.109), kind=kOutput, calls=%fused_computation.2.clone.1 | convolution fusion | flops 2516582400 | bytes 14909952 | tf_op jit(solution)/shard_map/while/body/eval_jaxpr/qac,qbd->acbd/dot_general | solution.py:40
  311.1 19.4 %fusion.27 = f32[8,5,10]{2,0,1:T(8,128)S(1)} fusion(f32[5,64,10,512]{3,1,2,0:T(8,128)} %fusion.26, bf16[8,8,64,512]{3,1,2,0:T(8,128)(2,1)} %get-tuple-element.118, s32[]{:T(128)} %get-tuple-element.109, f32[8,5,10]{2,0,1:T(8,128)S(1)} %get-tuple-element.110, pred[]{:T(512)S(6)} %compare.3), kind=kOutput, calls=%fused_computation.5.clone.1 | convolution fusion | flops 157287200 | bytes 7081601 | tf_op jit(solution)/shard_map/while/body/eval_jaxpr/pcd,acbd->pab/dot_general | solution.py:43
  330.5 0.1 reshape.11
  330.6 6.4 %all-reduce = f32[8,5,2,5]{3,2,0,1:T(2,128)S(1)} all-reduce(f32[8,5,2,5]{3,2,0,1:T(2,128)S(1)} %reshape.11), channel_id=2, replica_groups=mesh['pair'=2,'vblk'=16] {'pair'}, use_global_device_ids=true, to_apply=%region_2.3.clone | all-reduce | flops 400 | bytes 3200
  337.1 0.6 copy.17
  (2 shorter events, 0.0 us)
Async XLA Ops:
  6.5 8.9 %copy-start = (u32[32]{0:T(128)S(1)}, u32[32]{0:T(128)}, u32[]{:S(2)}) copy-start(u32[32]{0:T(128)} %constant.17) | copy-start | bytes 388
  6.5 90.7 %all-gather.2.cloned.1.call-start = ((), (), s32[]{:S(2)}) async-start(), calls=%async_computation | async-start | bytes 4325376 | tf_op jit(solution)/shard_map/all_gather | solution.py:29
  7.3 47.4 %collective-permute-start = (bf16[768,5,512]{2,0,1:T(8,128)(2,1)}, bf16[768,5,512]{2,0,1:T(8,128)(2,1)}, u32[]{:S(2)}, u32[]{:S(2)}) collective-permute-start(bf16[768,5,512]{2,0,1:T(8,128)(2,1)} %param.4), channel_id=1, source_target_pairs={{0,1},{1,2},{2,3},{3,4},{4,5},{5,6},{6,7},{7,8},{8,9},{9,10},{10,1... | collective-permute-start | bytes 11796488 | tf_op jit(solution)/shard_map/ppermute | solution.py:14
Sparse Core Ops, SparseCore 0:
  10.3 86.9 all-gather.1
where the time goes:
time: 349 us; the launch traced here: 345 us
  matrix products  227 us (65%)
  waiting for transfers between devices  74.1 us (21%)
  local copies, waits for them, and re-layouts  14.2 us (4%)
  between operations  14.1 us (4%)
  other arithmetic  7.06 us (2%)
  blocking collectives  6.45 us (2%)
    dot_general x8, matrix products, one_block(): jnp.einsum('pcd,acbd->pab', piece_part.astype(jnp.float32), integrals, pr...  155 us
    dot_general x8, matrix products, one_block(): jnp.einsum('qac,qbd->acbd', own_part, partner, preferred_element_type=jnp...  71.3 us
    ppermute x1, waiting for transfers between devices, shifted(): return lax.ppermute(value, axis, pairs)  37.9 us
    all_gather x1, waiting for transfers between devices, body(): amp_piece = lax.all_gather(amplitudes, ('pair', 'vblk'), axis=1, tiled=True)  35.5 us
    concatenate x1, other arithmetic, body(): partner = jnp.concatenate(collected, axis=1)  7.06 us
    unnamed x5, local copies, waits for them, and re-layouts  6.99 us
  transfers between devices with their start and end apart: 2, of which 2 were waited for; matrix products, arithmetic and copies ran while one was open for 4% of the time, Pallas kernels for 0%

commit v1 on v0

v1 whole, which is shorter than its diff:
```python
import functools
import math

import jax
import jax.numpy as jnp
from jax import lax
from jax.experimental import pallas as pl
from jax.experimental.pallas import tpu as pltpu
from jax.sharding import PartitionSpec as P

STEPS = 2
MESH = pl.DeviceIdType.MESH
F32 = jnp.float32
BF16 = jnp.bfloat16


def shifted(value, axis, steps):
    count = lax.axis_size(axis)
    pairs = [(source, (source + steps) % count) for source in range(count)]
    return lax.ppermute(value, axis, pairs)


def general_body(factors, amplitudes):
    aux_rows = factors.shape[0]
    block_rows = factors.shape[1]
    pair_count = amplitudes.shape[0]
    virtuals = amplitudes.shape[2]
    partner = jnp.concatenate([factors, shifted(factors, "vblk", 1)], axis=1)
    running = jnp.zeros((pair_count, block_rows, STEPS * block_rows), F32)
    amp_piece = lax.all_gather(amplitudes, ("pair", "vblk"), axis=1, tiled=True)
    row_count = amp_piece.shape[1]
    group_size = math.gcd(row_count, 64)
    block_count = row_count // group_size
    piece_blocks = amp_piece.reshape(pair_count, block_count, group_size, virtuals).transpose(
        1, 0, 2, 3
    )
    own_parts = factors.reshape(aux_rows, block_rows, block_count, group_size).transpose(2, 0, 1, 3)

    def one_block(carried, pieces):
        piece_part, own_part = pieces
        integrals = jnp.einsum("qac,qbd->acbd", own_part, partner, preferred_element_type=F32)
        update = jnp.einsum(
            "pcd,acbd->pab", piece_part.astype(F32), integrals, precision=lax.Precision.HIGHEST
        )
        return (carried + update, None)

    running, unused = lax.scan(one_block, running, (piece_blocks, own_parts))
    partial_ladder = running.reshape(pair_count, block_rows, STEPS, block_rows)
    return lax.psum_scatter(partial_ladder, "pair", scatter_dimension=0, tiled=True)


def kernel(dims, fac, amp, out, nb, fact, tall, wst, acc, red, part, recv, send, fsend, frecv, xs, xr):
    nx, nz, ny, nk = dims
    nv = nz * ny * nk
    blocks, aux, virt = fac.shape
    pairs, rows, _ = amp.shape
    group = 2 * rows
    groups = virt // group
    wide = 2 * pairs * rows

    x = lax.axis_index("pair")
    v = lax.axis_index("vblk")
    z, y, k = v // (ny * nk), (v // nk) % ny, v % nk

    def place(zz, yy, kk):
        return (zz * ny + yy) * nk + kk

    zs = [lax.rem(z + i, nz) for i in range(nz)]
    nxt, prv = lax.rem(v + 1, nv), lax.rem(v + nv - 1, nv)
    to_y, to_k = (x, place(z, 1 - y, k)), (x, place(z, y, 1 - k))
    to_x = (1 - x, v)

    barrier = pltpu.get_barrier_semaphore()
    peers = [(x, place(zz, y, k)) for zz in zs[1:]] + [to_y, to_k, to_x, (x, nxt), (x, prv)]
    for peer in peers:
        pl.semaphore_signal(barrier, inc=1, device_id=peer, device_id_type=MESH)
    pl.semaphore_wait(barrier, len(peers))

    sends = []

    def push(src, piece, target):
        copy = pltpu.make_async_remote_copy(
            src_ref=src,
            dst_ref=tall.at[piece],
            send_sem=send.at[len(sends)],
            recv_sem=recv.at[piece],
            device_id=target,
            device_id_type=MESH,
        )
        copy.start()
        sends.append(copy)

    def arrived(piece):
        pltpu.make_async_remote_copy(
            src_ref=amp,
            dst_ref=tall.at[piece],
            send_sem=send.at[0],
            recv_sem=recv.at[piece],
            device_id=to_x,
            device_id_type=MESH,
        ).wait_recv()

    def factor(j):
        return pltpu.make_async_remote_copy(
            src_ref=fac.at[j],
            dst_ref=nb.at[j],
            send_sem=fsend.at[j],
            recv_sem=frecv.at[j],
            device_id=(x, nxt),
            device_id_type=MESH,
        )

    mine = x * nv + v
    for zz in zs[1:]:
        push(amp, mine, (x, place(zz, y, k)))
    push(amp, mine, to_y)
    push(amp, mine, to_x)
    push(amp, mine, to_k)
    for j in range(blocks):
        factor(j).start()
    tall[pl.ds(mine, 1)] = amp[...][None]

    def stage_z():
        for zz in zs[1:]:
            piece = x * nv + place(zz, y, k)
            arrived(piece)
            for target in (to_y, to_x, to_k):
                push(tall.at[piece], piece, target)

    def stage_y():
        for zz in zs:
            piece = x * nv + place(zz, 1 - y, k)
            arrived(piece)
            for target in (to_x, to_k):
                push(tall.at[piece], piece, target)

    def stage_x(ys):
        for yy in ys:
            for zz in zs:
                piece = (1 - x) * nv + place(zz, yy, k)
                arrived(piece)
                push(tall.at[piece], piece, to_k)

    def stage_k():
        for xx in (x, 1 - x):
            for yy in (y, 1 - y):
                for zz in zs:
                    arrived(xx * nv + place(zz, yy, 1 - k))

    half = virt // 2

    def integrals(src, j):
        def one(i, _):
            a = i // 2
            start = pl.multiple_of(lax.rem(i, 2) * half, half)
            w = jnp.dot(
                fact[a, pl.ds(start, half), :], src[j], preferred_element_type=F32
            )
            high = w.astype(BF16)
            wst[j, 0, a, pl.ds(start, half), :] = high
            wst[j, 1, a, pl.ds(start, half), :] = (w - high.astype(F32)).astype(BF16)
            return 0

        lax.fori_loop(0, 2 * blocks, one, 0)

    def contract(s, j):
        acc[...] = jnp.zeros_like(acc)

        def one(g, _):
            lhs = wst[j, :, :, pl.ds(pl.multiple_of(g * group, group), group), :]
            lhs = lhs.reshape(2 * blocks * group, virt)
            rhs = tall[pl.ds(2 * g, 2)].reshape(wide, virt)
            acc[...] += lax.dot_general(
                lhs, rhs, (((1,), (1,)), ((), ())), preferred_element_type=F32
            )
            return 0

        lax.fori_loop(0, groups, one, 0)
        full = acc[...].reshape(2, blocks, group, wide)
        full = full[0] + full[1]
        row = lax.broadcasted_iota(jnp.int32, (blocks, group, wide), 1)
        col = lax.broadcasted_iota(jnp.int32, (blocks, group, wide), 2)
        own = (col // (pairs * rows)) * rows + col % rows
        red[s * blocks + j] = jnp.sum(jnp.where(row == own, full, 0.0), axis=1)

    def turn(a, _):
        fact[a] = fac[a].T
        return 0

    lax.fori_loop(0, blocks, turn, 0)
    integrals(fac, 0)
    integrals(fac, 1)
    stage_z()
    integrals(fac, 2)
    integrals(fac, 3)
    stage_y()
    integrals(fac, 4)
    stage_x([y])
    stage_x([1 - y])
    stage_k()
    for j in range(blocks):
        contract(0, j)
    for j in range(blocks):
        factor(j).wait_recv()
        integrals(nb, j)
        contract(1, j)

    swap = pltpu.make_async_remote_copy(
        src_ref=red, dst_ref=part, send_sem=xs, recv_sem=xr, device_id=to_x, device_id_type=MESH
    )
    swap.start()
    for copy in sends:
        copy.wait_send()
    for j in range(blocks):
        factor(j).wait_send()
    swap.wait()
    out[...] = red[...] + part[...]


def staged_body(dims, factors, amplitudes):
    aux, blocks, virt = factors.shape
    pairs, rows, _ = amplitudes.shape
    pieces = dims[0] * dims[1] * dims[2] * dims[3]
    wide = 2 * pairs * rows
    nsends = 3 * (dims[1] - 1) + (dims[1] + 2) + 2 * dims[1] + 2 * dims[1]
    vmem = pl.BlockSpec(memory_space=pltpu.VMEM)
    sums = pl.pallas_call(
        functools.partial(kernel, dims),
        out_shape=jax.ShapeDtypeStruct((STEPS * blocks, blocks, wide), F32),
        in_specs=[vmem, vmem],
        out_specs=vmem,
        scratch_shapes=[
            pltpu.VMEM((blocks, aux, virt), BF16),
            pltpu.VMEM((blocks, virt, aux), BF16),
            pltpu.VMEM((pieces, pairs, rows, virt), BF16),
            pltpu.VMEM((blocks, 2, blocks, virt, virt), BF16),
            pltpu.VMEM((2 * blocks * 2 * rows, wide), F32),
            pltpu.VMEM((STEPS * blocks, blocks, wide), F32),
            pltpu.VMEM((STEPS * blocks, blocks, wide), F32),
            pltpu.SemaphoreType.DMA((pieces,)),
            pltpu.SemaphoreType.DMA((pieces,)),
            pltpu.SemaphoreType.DMA((blocks,)),
            pltpu.SemaphoreType.DMA((blocks,)),
            pltpu.SemaphoreType.DMA,
            pltpu.SemaphoreType.DMA,
        ],
        compiler_params=pltpu.CompilerParams(
            collective_id=0, has_side_effects=True, vmem_limit_bytes=56 * 1024 * 1024
        ),
    )(factors.transpose(1, 0, 2), amplitudes)
    share = pairs // dims[0]
    sums = sums.reshape(STEPS, blocks, blocks, 2, pairs, rows).sum(axis=(3, 5))
    sums = sums.transpose(3, 2, 0, 1)
    return lax.dynamic_slice_in_dim(sums, lax.axis_index("pair") * share, share, 0)


def solution(mesh):
    placed = (P("pair", "vblk", None), P(None, ("pair", "vblk"), None))
    staged = mesh.shape["pair"] == 2 and mesh.shape["vblk"] == 16
    body = functools.partial(staged_body, (2, 4, 2, 2)) if staged else general_body
    return jax.shard_map(
        body, mesh=mesh, in_specs=placed, out_specs=P("pair", "vblk", None, None), check_vma=False
    )
```

time: 349 us -> 153 us (0.44); the launches traced: 345 us -> 153 us
  matrix products: 227 us -> 0 us
  Pallas kernels: 0 us -> 151 us
  waiting for transfers between devices: 74.1 us -> 0 us
  between operations: 14.1 us -> 0.03 us
  local copies, waits for them, and re-layouts: 14.2 us -> 1.88 us
  other arithmetic: 7.06 us -> 0.13 us
  blocking collectives: 6.45 us -> 0 us
    dot_general x16 -> x0, matrix products: 227 us -> none  [the longest x8 155 us: one_block(): jnp.einsum('pcd,acbd->pab', piece_part.astype(jnp.float32), integrals, pr...]
    pallas_call x0 -> x1, Pallas kernels: none -> 151 us  [staged_body(): pl.pallas_call(functools.partial(kernel, dims), out_shape=jax.ShapeDtypeS...]
    ppermute x1 -> x0, waiting for transfers between devices: 37.9 us -> none  [shifted(): return lax.ppermute(value, axis, pairs)]
    all_gather x1 -> x0, waiting for transfers between devices: 35.5 us -> none  [body(): amp_piece = lax.all_gather(amplitudes, ('pair', 'vblk'), axis=1, tiled=True)]
    concatenate x1 -> x0, other arithmetic: 7.06 us -> none  [body(): partner = jnp.concatenate(collected, axis=1)]
    unnamed x5 -> x0, local copies, waits for them, and re-layouts: 6.99 us -> none
    all_gather x1 -> x0, local copies, waits for them, and re-layouts: 6.5 us -> none  [body(): amp_piece = lax.all_gather(amplitudes, ('pair', 'vblk'), axis=1, tiled=True)]
    unnamed x1 -> x0, blocking collectives: 6.45 us -> none
  transfers between devices with their start and end apart: 2 -> 0, of which waited for: 2 -> 0; matrix products, arithmetic and copies ran while one was open for 4% -> 0% of each run, Pallas kernels for 0% -> 0%
where the time goes in v1:
time: 153 us
  Pallas kernels  151 us (99%)
  local copies, waits for them, and re-layouts  1.88 us (1%)
    pallas_call x1, Pallas kernels, staged_body(): pl.pallas_call(functools.partial(kernel, dims), out_shape=jax.ShapeDtypeS...  151 us

profile of v1, /device:TPU:15, one launch (start us, length us, event | category | flops | bytes accessed | tf_op | source)
XLA Modules:
  0.0 153.3 jit_solution(10709979806198874400)
XLA Ops:
  0.0 151.3 %shard_map.28 = f32[10,5,256]{2,1,0:T(8,128)} custom-call(bf16[5,768,512]{2,1,0:T(8,128)(2,1)} %bitcast.3, bf16[8,16,512]{2,1,0:T(8,128)(2,1)} %amp.1), custom_call_target="tpu_custom_call" | custom-call | tf_op jit(solution)/shard_map/pallas_call | solution.py:227
  151.3 1.0 reshape.3
  152.3 0.1 reduce_sum.9
  152.5 0.1 dynamic-slice_bitcast_fusion
  152.5 0.8 copy.3

commit v2 on v1

--- a/solution.py
+++ b/solution.py
@@ -49,7 +49,7 @@
     return lax.psum_scatter(partial_ladder, "pair", scatter_dimension=0, tiled=True)
 
 
-def kernel(dims, fac, amp, out, nb, fact, tall, wst, acc, red, part, recv, send, fsend, frecv, xs, xr):
+def kernel(dims, fac, amp, out, own, nb, fact, tall, tt, wst, red, part, recv, send, fsend, frecv, lsem, xs, xr):
     nx, nz, ny, nk = dims
     nv = nz * ny * nk
     blocks, aux, virt = fac.shape
@@ -110,14 +110,18 @@
             device_id_type=MESH,
         )
 
+    def load(j):
+        return pltpu.make_async_copy(fac.at[j], own.at[j], lsem.at[j])
+
     mine = x * nv + v
     for zz in zs[1:]:
         push(amp, mine, (x, place(zz, y, k)))
     push(amp, mine, to_y)
     push(amp, mine, to_x)
     push(amp, mine, to_k)
+    factor(0).start()
     for j in range(blocks):
-        factor(j).start()
+        load(j).start()
     tall[pl.ds(mine, 1)] = amp[...][None]
 
     def stage_z():
@@ -147,63 +151,67 @@
                 for zz in zs:
                     arrived(xx * nv + place(zz, yy, 1 - k))
 
-    half = virt // 2
-
-    def integrals(src, j):
-        def one(i, _):
-            a = i // 2
-            start = pl.multiple_of(lax.rem(i, 2) * half, half)
-            w = jnp.dot(
-                fact[a, pl.ds(start, half), :], src[j], preferred_element_type=F32
-            )
+    def integrals(src, j, slot):
+        def one(a, _):
+            w = jnp.dot(fact[a], src[j], preferred_element_type=F32)
             high = w.astype(BF16)
-            wst[j, 0, a, pl.ds(start, half), :] = high
-            wst[j, 1, a, pl.ds(start, half), :] = (w - high.astype(F32)).astype(BF16)
+            wst[slot, 0, a] = high
+            wst[slot, 1, a] = (w - high.astype(F32)).astype(BF16)
             return 0
 
-        lax.fori_loop(0, 2 * blocks, one, 0)
-
-    def contract(s, j):
-        acc[...] = jnp.zeros_like(acc)
-
-        def one(g, _):
-            lhs = wst[j, :, :, pl.ds(pl.multiple_of(g * group, group), group), :]
-            lhs = lhs.reshape(2 * blocks * group, virt)
-            rhs = tall[pl.ds(2 * g, 2)].reshape(wide, virt)
-            acc[...] += lax.dot_general(
-                lhs, rhs, (((1,), (1,)), ((), ())), preferred_element_type=F32
-            )
-            return 0
-
-        lax.fori_loop(0, groups, one, 0)
-        full = acc[...].reshape(2, blocks, group, wide)
+        lax.fori_loop(0, blocks, one, 0)
+
+    def contract(slot, panel):
+        lhs = jnp.concatenate(
+            [
+                wst[slot, :, :, g * group : (g + 1) * group, :].reshape(2 * blocks * group, virt)
+                for g in range(groups)
+            ],
+            axis=1,
+        )
+        rhs = tt[...].reshape(groups * virt, wide)
+        full = jnp.dot(lhs, rhs, preferred_element_type=F32).reshape(2, blocks, group, wide)
         full = full[0] + full[1]
         row = lax.broadcasted_iota(jnp.int32, (blocks, group, wide), 1)
         col = lax.broadcasted_iota(jnp.int32, (blocks, group, wide), 2)
-        own = (col // (pairs * rows)) * rows + col % rows
-        red[s * blocks + j] = jnp.sum(jnp.where(row == own, full, 0.0), axis=1)
+        diag = (col // (pairs * rows)) * rows + col % rows
+        red[panel] = jnp.sum(jnp.where(row == diag, full, 0.0), axis=1)
+
+    def contract_own(j, _):
+        contract(j, j)
+        return 0
+
+    def turn_amp(g, _):
+        tt[g] = tall[pl.ds(2 * g, 2)].reshape(wide, virt).T
+        return 0
 
     def turn(a, _):
-        fact[a] = fac[a].T
+        fact[a] = own[a].T
         return 0
 
+    for j in range(blocks):
+        load(j).wait()
     lax.fori_loop(0, blocks, turn, 0)
-    integrals(fac, 0)
-    integrals(fac, 1)
+    integrals(own, 0, 0)
+    integrals(own, 1, 1)
     stage_z()
-    integrals(fac, 2)
-    integrals(fac, 3)
+    for j in range(1, blocks):
+        factor(j).start()
+    for j in range(2, blocks):
+        integrals(own, j, j)
     stage_y()
-    integrals(fac, 4)
+    factor(0).wait_recv()
+    integrals(nb, 0, blocks)
     stage_x([y])
     stage_x([1 - y])
     stage_k()
-    for j in range(blocks):
-        contract(0, j)
-    for j in range(blocks):
+    lax.fori_loop(0, groups, turn_amp, 0)
+    lax.fori_loop(0, blocks, contract_own, 0)
+    contract(blocks, blocks)
+    for j in range(1, blocks):
         factor(j).wait_recv()
-        integrals(nb, j)
-        contract(1, j)
+        integrals(nb, j, j - 1)
+        contract(j - 1, blocks + j)
 
     swap = pltpu.make_async_remote_copy(
         src_ref=red, dst_ref=part, send_sem=xs, recv_sem=xr, device_id=to_x, device_id_type=MESH
@@ -227,25 +235,27 @@
     sums = pl.pallas_call(
         functools.partial(kernel, dims),
         out_shape=jax.ShapeDtypeStruct((STEPS * blocks, blocks, wide), F32),
-        in_specs=[vmem, vmem],
+        in_specs=[pl.BlockSpec(memory_space=pl.ANY), vmem],
         out_specs=vmem,
         scratch_shapes=[
             pltpu.VMEM((blocks, aux, virt), BF16),
+            pltpu.VMEM((blocks, aux, virt), BF16),
             pltpu.VMEM((blocks, virt, aux), BF16),
             pltpu.VMEM((pieces, pairs, rows, virt), BF16),
-            pltpu.VMEM((blocks, 2, blocks, virt, virt), BF16),
-            pltpu.VMEM((2 * blocks * 2 * rows, wide), F32),
+            pltpu.VMEM((virt // (2 * rows), virt, wide), BF16),
+            pltpu.VMEM((blocks + 1, 2, blocks, virt, virt), BF16),
             pltpu.VMEM((STEPS * blocks, blocks, wide), F32),
             pltpu.VMEM((STEPS * blocks, blocks, wide), F32),
             pltpu.SemaphoreType.DMA((pieces,)),
             pltpu.SemaphoreType.DMA((pieces,)),
             pltpu.SemaphoreType.DMA((blocks,)),
             pltpu.SemaphoreType.DMA((blocks,)),
+            pltpu.SemaphoreType.DMA((blocks,)),
             pltpu.SemaphoreType.DMA,
             pltpu.SemaphoreType.DMA,
         ],
         compiler_params=pltpu.CompilerParams(
-            collective_id=0, has_side_effects=True, vmem_limit_bytes=56 * 1024 * 1024
+            collective_id=0, has_side_effects=True, vmem_limit_bytes=60 * 1024 * 1024
         ),
     )(factors.transpose(1, 0, 2), amplitudes)
     share = pairs // dims[0]

time: 153 us -> 117 us (0.76)
  Pallas kernels: 151 us -> 115 us
    pallas_call x1, Pallas kernels: 151 us -> 115 us  [staged_body(): pl.pallas_call(functools.partial(kernel, dims), out_shape=jax.ShapeDtypeS...]
where the time goes in v2:
time: 117 us
  Pallas kernels  115 us (98%)
  local copies, waits for them, and re-layouts  1.88 us (2%)
    pallas_call x1, Pallas kernels, staged_body(): pl.pallas_call(functools.partial(kernel, dims), out_shape=jax.ShapeDtypeS...  115 us

profile of v2, /device:TPU:15, one launch (start us, length us, event | category | flops | bytes accessed | tf_op | source)
XLA Modules:
  0.0 116.9 jit_solution(18120640041379433189)
XLA Ops:
  0.0 114.8 %shard_map.28 = f32[10,5,256]{2,1,0:T(8,128)} custom-call(bf16[5,768,512]{2,1,0:T(8,128)(2,1)} %bitcast.3, bf16[8,16,512]{2,1,0:T(8,128)(2,1)} %amp.1), custom_call_target="tpu_custom_call" | custom-call | tf_op jit(solution)/shard_map/pallas_call | solution.py:235
  114.8 1.0 reshape.3
  115.9 0.1 reduce_sum.9
  116.0 0.1 dynamic-slice_bitcast_fusion
  116.1 0.8 copy.3

commit v3 on v2

--- a/solution.py
+++ b/solution.py
@@ -195,8 +195,6 @@
     integrals(own, 0, 0)
     integrals(own, 1, 1)
     stage_z()
-    for j in range(1, blocks):
-        factor(j).start()
     for j in range(2, blocks):
         integrals(own, j, j)
     stage_y()
@@ -204,6 +202,8 @@
     integrals(nb, 0, blocks)
     stage_x([y])
     stage_x([1 - y])
+    for j in range(1, blocks):
+        factor(j).start()
     stage_k()
     lax.fori_loop(0, groups, turn_amp, 0)
     lax.fori_loop(0, blocks, contract_own, 0)

time: 117 us -> 93.5 us (0.80)
  the two profiles are of different devices: /device:TPU:15 before, /device:TPU:18 now
where the time goes in v3:
time: 93.5 us; the launch traced here: 93.3 us
  Pallas kernels  91.3 us (98%)
  local copies, waits for them, and re-layouts  1.88 us (2%)
    pallas_call x1, Pallas kernels, staged_body(): pl.pallas_call(functools.partial(kernel, dims), out_shape=jax.ShapeDtypeS...  91.3 us

profile of v3, /device:TPU:18, one launch (start us, length us, event | category | flops | bytes accessed | tf_op | source)
XLA Modules:
  0.0 93.3 jit_solution(14217669296932543630)
XLA Ops:
  0.0 91.3 %shard_map.28 = f32[10,5,256]{2,1,0:T(8,128)} custom-call(bf16[5,768,512]{2,1,0:T(8,128)(2,1)} %bitcast.3, bf16[8,16,512]{2,1,0:T(8,128)(2,1)} %amp.1), custom_call_target="tpu_custom_call" | custom-call | tf_op jit(solution)/shard_map/pallas_call | solution.py:235
  91.3 1.0 %reshape.3 = f32[2,5,5,2,8,16]{5,4,3,2,1,0:T(8,128)S(1)} reshape(f32[10,5,256]{2,1,0:T(8,128)} %shard_map.28) | data formatting | bytes 102400 | tf_op jit(solution)/shard_map/reshape | solution.py:262
  92.3 0.1 reduce_sum.9
  92.5 0.1 dynamic-slice_bitcast_fusion
  92.6 0.8 copy.3
